TPU v7x, 32 devices: a whole 2x2x4 slice. The times are simulated.
32 devices in a mesh: grp: 4 (over y, core), ex: 2 (over x), tp: 4 (over z).
Axes of the slice: x: 2, y: 2, z: 4, core: 2. Of those that a mesh axis runs over, the one named last changes fastest.
Arguments:
- residual: bfloat16 [128, 2, 6144], P(('grp', 'ex'), None, 'tp'), may hold values from -34 to 34
- query_new: bfloat16 [128, 2, 6144], P(('grp', 'ex'), None, 'tp'), may hold values from -5 to 5
- key_new: bfloat16 [128, 2, 1024], P(('grp', 'ex'), None, 'tp'), may hold values from -8 to 8
- value_new: bfloat16 [128, 2, 1024], P(('grp', 'ex'), None, 'tp'), may hold values from -12 to 12
- key_cache: bfloat16 [128, 8, 512, 128], P(('grp', 'ex'), 'tp'), may hold values from -5 to 5
- value_cache: bfloat16 [128, 8, 512, 128], P(('grp', 'ex'), 'tp'), may hold values from -12 to 12
- lengths: int32 [128], P(('grp', 'ex')), may hold values from 128 to 512, as said below
- norm_gain: bfloat16 [6144], P('tp'), may hold values from 0.099609375 to 1.8984375
- router: float32 [6144, 8], P('tp'), may hold values from -0.078125 to 0.078125
- routes: int32 [128, 2, 2], P(('grp', 'ex')), may hold values from 0 to 7, all different within a row; in each aligned block of 32 rows (0 to 31, 32 to 63, ..., all dimensions but the last counted through in order) at most 16 rows name the same one
- w_gate: bfloat16 [8, 6144, 8192], P('ex', None, ('grp', 'tp')), may hold values from -0.078125 to 0.078125
- w_up: bfloat16 [8, 6144, 8192], P('ex', None, ('grp', 'tp')), may hold values from -0.078125 to 0.078125
- w_down: bfloat16 [8, 8192, 6144], P('ex', ('grp', 'tp')), may hold values from -0.09375 to 0.09375
Outputs:
- attended: bfloat16 [128, 2, 6144], P(('grp', 'ex'), None, 'tp')
- expert_mix: bfloat16 [128, 2, 6144], P(('grp', 'ex'), None, 'tp')
Inputs may be any that keep to these rules, and one draw needn't show every extreme that they name: `routes`: over the rows of one device (aligned blocks of 32 rows, environments then steps) no expert is named more than 16 times, and in some blocks one is named exactly 16 times; a row's two experts differ. `lengths`: some environment's cache is full.
All inputs are finite; a program needn't handle non-finite values.
Results may differ from a plain program's by a relative error of at most 0.023.
Values may be sent and summed in bfloat16 or wider, within the bound.
A program may use at most 192 MiB of HBM per device.

v0:
```python
import jax
import jax.numpy as jnp
from jax import lax
from jax.sharding import PartitionSpec as P

CAP = 16


def attend(query_new, key_new, value_new, key_cache, value_cache, lengths):
    env_count, step_count, feature_count = query_new.shape
    kv_count = key_cache.shape[1]
    context = key_cache.shape[2]
    head_dim = key_cache.shape[3]
    group_size = feature_count // (kv_count * head_dim)
    queries = query_new.reshape(env_count, step_count, kv_count, group_size, head_dim)
    keys_now = key_new.reshape(env_count, step_count, kv_count, head_dim)
    values_now = value_new.reshape(env_count, step_count, kv_count, head_dim)
    score_scale = head_dim ** (-0.5)
    cached = (
        jnp.einsum("eskgd,ekcd->eskgc", queries, key_cache, preferred_element_type=jnp.float32)
        * score_scale
    )
    fresh_scores = (
        jnp.einsum("eskgd,etkd->eskgt", queries, keys_now, preferred_element_type=jnp.float32)
        * score_scale
    )
    valid_mask = (lax.broadcasted_iota(jnp.int32, (env_count, context), 1) < lengths[:, None])[
        :, None, None, None, :
    ]
    causal = (
        lax.broadcasted_iota(jnp.int32, (step_count, step_count), 1)
        <= lax.broadcasted_iota(jnp.int32, (step_count, step_count), 0)
    )[None, :, None, None, :]
    cached = jnp.where(valid_mask, cached, -1e30)
    fresh_scores = jnp.where(causal, fresh_scores, -1e30)
    row_top = jnp.maximum(jnp.max(cached, -1), jnp.max(fresh_scores, -1))[..., None]
    weight_cached = jnp.where(valid_mask, jnp.exp(cached - row_top), 0.0)
    weight_fresh = jnp.where(causal, jnp.exp(fresh_scores - row_top), 0.0)
    row_total = (jnp.sum(weight_cached, -1) + jnp.sum(weight_fresh, -1))[..., None]
    probs_cached = (weight_cached / row_total).astype(jnp.bfloat16)
    probs_fresh = (weight_fresh / row_total).astype(jnp.bfloat16)
    heads_out = jnp.einsum(
        "eskgc,ekcd->eskgd", probs_cached, value_cache, preferred_element_type=jnp.float32
    )
    heads_out = heads_out + jnp.einsum(
        "eskgt,etkd->eskgd", probs_fresh, values_now, preferred_element_type=jnp.float32
    )
    return heads_out.reshape(env_count, step_count, feature_count)


def add_group(totals, addition, group_at):
    current = lax.dynamic_slice_in_dim(totals, group_at, 1, 1)
    return lax.dynamic_update_slice_in_dim(totals, current + addition[:, None], group_at, 1)


def per_device(
    residual,
    query_new,
    key_new,
    value_new,
    key_cache,
    value_cache,
    lengths,
    norm_gain,
    router,
    routes,
    w_gate,
    w_up,
    w_down,
):
    env_count, step_count, slice_width = residual.shape
    local_experts, width, hidden_local = w_gate.shape
    experts = router.shape[1]
    topk = routes.shape[2]
    group_count = lax.axis_size("grp")
    tensor_count = lax.axis_size("tp")
    owner_count = lax.axis_size("ex")
    row_count = env_count * step_count
    state = residual.astype(jnp.float32) + attend(
        query_new, key_new, value_new, key_cache, value_cache, lengths
    )
    attended = state.astype(jnp.bfloat16)
    squares = jnp.sum(state * state, -1)
    scaled = state * norm_gain.astype(jnp.float32)
    partial_logits = jnp.einsum("esd,dx->esx", scaled, router, precision=lax.Precision.HIGHEST)
    squares, logits = lax.psum((squares, partial_logits), "tp")
    root_mean = jnp.sqrt(squares / width + 1e-05)[..., None]
    logits = logits / root_mean
    normed = (scaled / root_mean).astype(jnp.bfloat16)
    expert_ids = lax.broadcasted_iota(jnp.int32, (1, 1, 1, experts), 3)
    picked_logits = jnp.sum(
        jnp.where(routes[..., None] == expert_ids, logits[:, :, None, :], 0.0), -1
    )
    first_gate = 1.0 / (1.0 + jnp.exp(picked_logits[..., 1] - picked_logits[..., 0]))
    second_gate = 1.0 - first_gate
    flat_routes = routes.reshape(row_count * topk)
    expert_hits = (flat_routes[:, None] == lax.broadcasted_iota(jnp.int32, (1, experts), 1)).astype(
        jnp.int32
    )
    earlier = jnp.cumsum(expert_hits, axis=0) - expert_hits
    slot_ids = jnp.sum(earlier * expert_hits, axis=1)
    targets = flat_routes * CAP + slot_ids
    slot_table = lax.broadcasted_iota(jnp.int32, (1, experts * CAP), 1)
    placed = (
        (targets[:, None] == slot_table)
        .astype(jnp.bfloat16)
        .reshape(row_count, topk, experts * CAP)
    )
    sender = jnp.sum(placed, axis=1)
    gate_init = jnp.zeros((local_experts, group_count, owner_count, CAP, hidden_local), jnp.float32)
    packed = jnp.einsum(
        "rs,rd->sd",
        sender,
        normed.reshape(row_count, slice_width),
        preferred_element_type=jnp.float32,
    )
    outgoing = packed.astype(jnp.bfloat16).reshape(experts, CAP, slice_width)
    received = lax.all_to_all(outgoing, "ex", split_axis=0, concat_axis=0, tiled=True)
    received = received.reshape(1, owner_count, local_experts, CAP, slice_width)
    pieces = lax.all_gather(received, ("grp", "tp"), axis=0, tiled=True)

    def add_block(position, running):
        block = lax.dynamic_index_in_dim(pieces, position, 0, keepdims=False)
        group_at = position // tensor_count
        column_at = position % tensor_count
        gate_rows = lax.dynamic_slice_in_dim(w_gate, column_at * slice_width, slice_width, 1)
        up_rows = lax.dynamic_slice_in_dim(w_up, column_at * slice_width, slice_width, 1)
        gate_add = jnp.einsum(
            "ajcd,jdf->jacf", block, gate_rows, preferred_element_type=jnp.float32
        )
        up_add = jnp.einsum("ajcd,jdf->jacf", block, up_rows, preferred_element_type=jnp.float32)
        return (add_group(running[0], gate_add, group_at), add_group(running[1], up_add, group_at))

    gate_sums, up_sums = lax.fori_loop(0, pieces.shape[0], add_block, (gate_init, gate_init))
    hidden = (jax.nn.silu(gate_sums) * up_sums).astype(jnp.bfloat16)
    down_split = w_down.reshape(local_experts, hidden_local, tensor_count, slice_width)
    down_terms = jnp.einsum(
        "jgacf,jftd->gtajcd", hidden, down_split, preferred_element_type=jnp.float32
    )
    down_terms = down_terms.reshape(
        group_count * tensor_count, owner_count, local_experts, CAP, slice_width
    )
    summed = lax.psum_scatter(
        down_terms.astype(jnp.bfloat16), ("grp", "tp"), scatter_dimension=0, tiled=True
    ).astype(jnp.float32)
    returned = lax.all_to_all(
        summed[0].astype(jnp.bfloat16), "ex", split_axis=0, concat_axis=0, tiled=True
    )
    returned = returned.reshape(experts * CAP, slice_width)
    picked_rows = jnp.einsum("rks,sd->rkd", placed, returned, preferred_element_type=jnp.float32)
    picked_rows = picked_rows.reshape(env_count, step_count, topk, slice_width)
    expert_mix = (
        first_gate[..., None] * picked_rows[:, :, 0] + second_gate[..., None] * picked_rows[:, :, 1]
    )
    return (attended, expert_mix.astype(jnp.bfloat16))


def solution(mesh):
    return jax.shard_map(
        per_device,
        mesh=mesh,
        in_specs=(
            P(("grp", "ex"), None, "tp"),
            P(("grp", "ex"), None, "tp"),
            P(("grp", "ex"), None, "tp"),
            P(("grp", "ex"), None, "tp"),
            P(("grp", "ex"), "tp", None, None),
            P(("grp", "ex"), "tp", None, None),
            P(("grp", "ex")),
            P("tp"),
            P("tp", None),
            P(("grp", "ex"), None, None),
            P("ex", None, ("grp", "tp")),
            P("ex", None, ("grp", "tp")),
            P("ex", ("grp", "tp"), None),
        ),
        out_specs=(P(("grp", "ex"), None, "tp"), P(("grp", "ex"), None, "tp")),
        check_vma=False,
    )
```

profile of v0, /device:TPU:0, one launch (start us, length us, event | category | flops | bytes accessed | tf_op | source)
XLA Modules:
  0.0 363.5 jit_solution(15550605077625567425)
XLA Ops:
  18.5 13.9 %all-reduce = (f32[16,2]{0,1:T(2,128)S(1)}, f32[16,2,8]{0,2,1:T(8,128)S(1)}) all-reduce(f32[16,2]{0,1:T(2,128)S(1)} %multiply_reduce_fusion, f32[16,2,8]{0,2,1:T(8,128)S(1)} %fusion.62), channel_id=1, replica_groups=mesh['grp'=4,'ex'=2,'tp'=4] {'tp'}, use_global_device_ids=true, to_apply=%region_6.7 | all-reduce | flops 288 | bytes 2304 | tf_op jit(solution)/shard_map/psum | solution.py:86
  33.9 9.0 %all_to_all.10 = bf16[8,16,1536]{2,1,0:T(8,128)(2,1)} all-to-all(bf16[8,16,1536]{2,1,0:T(8,128)(2,1)S(1)} %bitcast.148), channel_id=1, replica_groups=mesh['grp'=4,'ex'=2,'tp'=4] {'ex'}, dimensions={0} | all-to-all | bytes 786432 | tf_op jit(solution)/shard_map/all_to_all | solution.py:118
  43.2 49.2 %reshape.133 = bf16[4,512,4,1536]{3,2,1,0:T(4,128)(2,1)} reshape(bf16[4,512,6144]{2,1,0:T(8,128)(2,1)} %param.27) | data formatting | bytes 50331648 | tf_op jit(solution)/shard_map/reshape | solution.py:136
  92.4 9.8 %all-gather.2.cloned.1.call-done = bf16[16,2,4,16,1536]{4,3,2,1,0:T(8,128)(2,1)} async-done(((bf16[1,2,4,16,1536]{4,3,2,1,0:T(8,128)(2,1)}), bf16[16,2,4,16,1536]{4,3,2,1,0:T(8,128)(2,1)}) %all-gather.2.cloned.1.call-update) | async-done | bytes 6291472 | tf_op jit(solution)/shard_map/all_gather | solution.py:120
  102.5 128.9 %while.17 = (s32[]{:T(128)}, f32[4,4,2,16,512]{4,3,2,0,1:T(8,128)S(1)}, f32[4,4,2,16,512]{4,3,2,0,1:T(8,128)S(1)}, bf16[16,2,4,16,1536]{4,3,2,1,0:T(8,128)(2,1)}...) while((s32[]{:T(128)}, ...), condition=%wide.region_12.13_spmd, body=%wide.region_11.12_spmd.sunk | while | flops 402784256 | bytes 14419288 | solution.py:134
  102.5 4.0 %fusion.96 = f32[4,4,2,16,512]{4,3,2,0,1:T(8,128)S(1)} fusion(f32[4,4,2,16,512]{4,3,2,0,1:T(8,128)S(1)} %get-tuple-element.271, s32[]{:T(128)S(6)} %select_n.114, bf16[4,6144,512]{2,1,0:T(8,128)(2,1)} %get-tuple-element.288, s32[]{:T(128)S(6)} %select_n.116, bf16[16,2,4,16,1536]{4,3,2,1,0:T(8,128)(2,1)} %get-tuple-element.286, s32[]{:T(128)} %get-tuple-element.269), kind=kOutput, calls=%fused_computation.9.clone.1 | convolution fusion | flops 201392128 | bytes 7209480 | tf_op jit(solution)/shard_map/while/body/eval_jaxpr/ajcd,jdf->jacf/dot_general | solution.py:131
  106.5 4.0 %fusion.95 = f32[4,4,2,16,512]{4,3,2,0,1:T(8,128)S(1)} fusion(f32[4,4,2,16,512]{4,3,2,0,1:T(8,128)S(1)} %get-tuple-element.270, s32[]{:T(128)S(6)} %select_n.114, bf16[4,6144,512]{2,1,0:T(8,128)(2,1)} %get-tuple-element.287, s32[]{:T(128)S(6)} %select_n.116, bf16[16,2,4,16,1536]{4,3,2,1,0:T(8,128)(2,1)} %get-tuple-element.286, s32[]{:T(128)} %get-tuple-element.269), kind=kOutput, calls=%fused_computation.11.clone.1 | convolution fusion | flops 201392128 | bytes 7209480 | tf_op jit(solution)/shard_map/while/body/eval_jaxpr/ajcd,jdf->jacf/dot_general | solution.py:128
  110.6 4.0 %fusion.96 = f32[4,4,2,16,512]{4,3,2,0,1:T(8,128)S(1)} fusion(f32[4,4,2,16,512]{4,3,2,0,1:T(8,128)S(1)} %get-tuple-element.271, s32[]{:T(128)S(6)} %select_n.114, bf16[4,6144,512]{2,1,0:T(8,128)(2,1)} %get-tuple-element.288, s32[]{:T(128)S(6)} %select_n.116, bf16[16,2,4,16,1536]{4,3,2,1,0:T(8,128)(2,1)} %get-tuple-element.286, s32[]{:T(128)} %get-tuple-element.269), kind=kOutput, calls=%fused_computation.9.clone.1 | convolution fusion | flops 201392128 | bytes 7209480 | tf_op jit(solution)/shard_map/while/body/eval_jaxpr/ajcd,jdf->jacf/dot_general | solution.py:131
  114.6 4.0 %fusion.95 = f32[4,4,2,16,512]{4,3,2,0,1:T(8,128)S(1)} fusion(f32[4,4,2,16,512]{4,3,2,0,1:T(8,128)S(1)} %get-tuple-element.270, s32[]{:T(128)S(6)} %select_n.114, bf16[4,6144,512]{2,1,0:T(8,128)(2,1)} %get-tuple-element.287, s32[]{:T(128)S(6)} %select_n.116, bf16[16,2,4,16,1536]{4,3,2,1,0:T(8,128)(2,1)} %get-tuple-element.286, s32[]{:T(128)} %get-tuple-element.269), kind=kOutput, calls=%fused_computation.11.clone.1 | convolution fusion | flops 201392128 | bytes 7209480 | tf_op jit(solution)/shard_map/while/body/eval_jaxpr/ajcd,jdf->jacf/dot_general | solution.py:128
  118.6 4.0 %fusion.96 = f32[4,4,2,16,512]{4,3,2,0,1:T(8,128)S(1)} fusion(f32[4,4,2,16,512]{4,3,2,0,1:T(8,128)S(1)} %get-tuple-element.271, s32[]{:T(128)S(6)} %select_n.114, bf16[4,6144,512]{2,1,0:T(8,128)(2,1)} %get-tuple-element.288, s32[]{:T(128)S(6)} %select_n.116, bf16[16,2,4,16,1536]{4,3,2,1,0:T(8,128)(2,1)} %get-tuple-element.286, s32[]{:T(128)} %get-tuple-element.269), kind=kOutput, calls=%fused_computation.9.clone.1 | convolution fusion | flops 201392128 | bytes 7209480 | tf_op jit(solution)/shard_map/while/body/eval_jaxpr/ajcd,jdf->jacf/dot_general | solution.py:131
  126.7 4.0 %fusion.96 = f32[4,4,2,16,512]{4,3,2,0,1:T(8,128)S(1)} fusion(f32[4,4,2,16,512]{4,3,2,0,1:T(8,128)S(1)} %get-tuple-element.271, s32[]{:T(128)S(6)} %select_n.114, bf16[4,6144,512]{2,1,0:T(8,128)(2,1)} %get-tuple-element.288, s32[]{:T(128)S(6)} %select_n.116, bf16[16,2,4,16,1536]{4,3,2,1,0:T(8,128)(2,1)} %get-tuple-element.286, s32[]{:T(128)} %get-tuple-element.269), kind=kOutput, calls=%fused_computation.9.clone.1 | convolution fusion | flops 201392128 | bytes 7209480 | tf_op jit(solution)/shard_map/while/body/eval_jaxpr/ajcd,jdf->jacf/dot_general | solution.py:131
  130.7 4.0 %fusion.95 = f32[4,4,2,16,512]{4,3,2,0,1:T(8,128)S(1)} fusion(f32[4,4,2,16,512]{4,3,2,0,1:T(8,128)S(1)} %get-tuple-element.270, s32[]{:T(128)S(6)} %select_n.114, bf16[4,6144,512]{2,1,0:T(8,128)(2,1)} %get-tuple-element.287, s32[]{:T(128)S(6)} %select_n.116, bf16[16,2,4,16,1536]{4,3,2,1,0:T(8,128)(2,1)} %get-tuple-element.286, s32[]{:T(128)} %get-tuple-element.269), kind=kOutput, calls=%fused_computation.11.clone.1 | convolution fusion | flops 201392128 | bytes 7209480 | tf_op jit(solution)/shard_map/while/body/eval_jaxpr/ajcd,jdf->jacf/dot_general | solution.py:128
  134.7 4.0 %fusion.96 = f32[4,4,2,16,512]{4,3,2,0,1:T(8,128)S(1)} fusion(f32[4,4,2,16,512]{4,3,2,0,1:T(8,128)S(1)} %get-tuple-element.271, s32[]{:T(128)S(6)} %select_n.114, bf16[4,6144,512]{2,1,0:T(8,128)(2,1)} %get-tuple-element.288, s32[]{:T(128)S(6)} %select_n.116, bf16[16,2,4,16,1536]{4,3,2,1,0:T(8,128)(2,1)} %get-tuple-element.286, s32[]{:T(128)} %get-tuple-element.269), kind=kOutput, calls=%fused_computation.9.clone.1 | convolution fusion | flops 201392128 | bytes 7209480 | tf_op jit(solution)/shard_map/while/body/eval_jaxpr/ajcd,jdf->jacf/dot_general | solution.py:131
  138.7 4.0 %fusion.95 = f32[4,4,2,16,512]{4,3,2,0,1:T(8,128)S(1)} fusion(f32[4,4,2,16,512]{4,3,2,0,1:T(8,128)S(1)} %get-tuple-element.270, s32[]{:T(128)S(6)} %select_n.114, bf16[4,6144,512]{2,1,0:T(8,128)(2,1)} %get-tuple-element.287, s32[]{:T(128)S(6)} %select_n.116, bf16[16,2,4,16,1536]{4,3,2,1,0:T(8,128)(2,1)} %get-tuple-element.286, s32[]{:T(128)} %get-tuple-element.269), kind=kOutput, calls=%fused_computation.11.clone.1 | convolution fusion | flops 201392128 | bytes 7209480 | tf_op jit(solution)/shard_map/while/body/eval_jaxpr/ajcd,jdf->jacf/dot_general | solution.py:128
  142.8 4.0 %fusion.96 = f32[4,4,2,16,512]{4,3,2,0,1:T(8,128)S(1)} fusion(f32[4,4,2,16,512]{4,3,2,0,1:T(8,128)S(1)} %get-tuple-element.271, s32[]{:T(128)S(6)} %select_n.114, bf16[4,6144,512]{2,1,0:T(8,128)(2,1)} %get-tuple-element.288, s32[]{:T(128)S(6)} %select_n.116, bf16[16,2,4,16,1536]{4,3,2,1,0:T(8,128)(2,1)} %get-tuple-element.286, s32[]{:T(128)} %get-tuple-element.269), kind=kOutput, calls=%fused_computation.9.clone.1 | convolution fusion | flops 201392128 | bytes 7209480 | tf_op jit(solution)/shard_map/while/body/eval_jaxpr/ajcd,jdf->jacf/dot_general | solution.py:131
  146.8 4.0 %fusion.95 = f32[4,4,2,16,512]{4,3,2,0,1:T(8,128)S(1)} fusion(f32[4,4,2,16,512]{4,3,2,0,1:T(8,128)S(1)} %get-tuple-element.270, s32[]{:T(128)S(6)} %select_n.114, bf16[4,6144,512]{2,1,0:T(8,128)(2,1)} %get-tuple-element.287, s32[]{:T(128)S(6)} %select_n.116, bf16[16,2,4,16,1536]{4,3,2,1,0:T(8,128)(2,1)} %get-tuple-element.286, s32[]{:T(128)} %get-tuple-element.269), kind=kOutput, calls=%fused_computation.11.clone.1 | convolution fusion | flops 201392128 | bytes 7209480 | tf_op jit(solution)/shard_map/while/body/eval_jaxpr/ajcd,jdf->jacf/dot_general | solution.py:128
  154.8 4.0 %fusion.95 = f32[4,4,2,16,512]{4,3,2,0,1:T(8,128)S(1)} fusion(f32[4,4,2,16,512]{4,3,2,0,1:T(8,128)S(1)} %get-tuple-element.270, s32[]{:T(128)S(6)} %select_n.114, bf16[4,6144,512]{2,1,0:T(8,128)(2,1)} %get-tuple-element.287, s32[]{:T(128)S(6)} %select_n.116, bf16[16,2,4,16,1536]{4,3,2,1,0:T(8,128)(2,1)} %get-tuple-element.286, s32[]{:T(128)} %get-tuple-element.269), kind=kOutput, calls=%fused_computation.11.clone.1 | convolution fusion | flops 201392128 | bytes 7209480 | tf_op jit(solution)/shard_map/while/body/eval_jaxpr/ajcd,jdf->jacf/dot_general | solution.py:128
  166.9 4.0 %fusion.96 = f32[4,4,2,16,512]{4,3,2,0,1:T(8,128)S(1)} fusion(f32[4,4,2,16,512]{4,3,2,0,1:T(8,128)S(1)} %get-tuple-element.271, s32[]{:T(128)S(6)} %select_n.114, bf16[4,6144,512]{2,1,0:T(8,128)(2,1)} %get-tuple-element.288, s32[]{:T(128)S(6)} %select_n.116, bf16[16,2,4,16,1536]{4,3,2,1,0:T(8,128)(2,1)} %get-tuple-element.286, s32[]{:T(128)} %get-tuple-element.269), kind=kOutput, calls=%fused_computation.9.clone.1 | convolution fusion | flops 201392128 | bytes 7209480 | tf_op jit(solution)/shard_map/while/body/eval_jaxpr/ajcd,jdf->jacf/dot_general | solution.py:131
  171.0 4.0 %fusion.95 = f32[4,4,2,16,512]{4,3,2,0,1:T(8,128)S(1)} fusion(f32[4,4,2,16,512]{4,3,2,0,1:T(8,128)S(1)} %get-tuple-element.270, s32[]{:T(128)S(6)} %select_n.114, bf16[4,6144,512]{2,1,0:T(8,128)(2,1)} %get-tuple-element.287, s32[]{:T(128)S(6)} %select_n.116, bf16[16,2,4,16,1536]{4,3,2,1,0:T(8,128)(2,1)} %get-tuple-element.286, s32[]{:T(128)} %get-tuple-element.269), kind=kOutput, calls=%fused_computation.11.clone.1 | convolution fusion | flops 201392128 | bytes 7209480 | tf_op jit(solution)/shard_map/while/body/eval_jaxpr/ajcd,jdf->jacf/dot_general | solution.py:128
  179.0 4.0 %fusion.95 = f32[4,4,2,16,512]{4,3,2,0,1:T(8,128)S(1)} fusion(f32[4,4,2,16,512]{4,3,2,0,1:T(8,128)S(1)} %get-tuple-element.270, s32[]{:T(128)S(6)} %select_n.114, bf16[4,6144,512]{2,1,0:T(8,128)(2,1)} %get-tuple-element.287, s32[]{:T(128)S(6)} %select_n.116, bf16[16,2,4,16,1536]{4,3,2,1,0:T(8,128)(2,1)} %get-tuple-element.286, s32[]{:T(128)} %get-tuple-element.269), kind=kOutput, calls=%fused_computation.11.clone.1 | convolution fusion | flops 201392128 | bytes 7209480 | tf_op jit(solution)/shard_map/while/body/eval_jaxpr/ajcd,jdf->jacf/dot_general | solution.py:128
  231.4 24.6 %convert_bitcast_fusion = bf16[4,4,2,4,16,1536]{5,4,1,2,0,3:T(8,128)(2,1)} fusion(bf16[4,512,4,1536,1,1]{3,2,1,0,5,4:T(4,128)(2,1)} %bitcast.144, f32[4,4,2,16,512]{4,3,2,0,1:T(8,128)S(1)} %get-tuple-element.161, f32[4,4,2,16,512]{4,3,2,0,1:T(8,128)S(1)} %get-tuple-element.160), kind=kOutput, calls=%fused_computation.18 | convolution fusion | flops 3225944064 | bytes 33554432 | tf_op jit(solution)/shard_map/jgacf,jftd->gtajcd/dot_general | solution.py:137
  256.0 6.1 %copy.111 = bf16[4,4,2,4,16,1536]{5,4,3,2,1,0:T(8,128)(2,1)} copy(bf16[4,4,2,4,16,1536]{5,4,1,2,0,3:T(8,128)(2,1)} %convert_bitcast_fusion) | data formatting | bytes 12582912 | tf_op jit(solution)/shard_map/convert_element_type | solution.py:144
  263.0 83.1 %reduce-scatter.2.cloned.1.call-done = bf16[1,2,4,16,1536]{4,3,2,1,0:T(8,128)(2,1)} async-done(((bf16[16,2,4,16,1536]{4,3,2,1,0:T(8,128)(2,1)}), bf16[1,2,4,16,1536]{4,3,2,1,0:T(8,128)(2,1)}) %reduce-scatter.2.cloned.1.call-update) | async-done | bytes 393232 | tf_op jit(solution)/shard_map/reduce_scatter | solution.py:143
  349.6 6.1 %all-to-all-done.1 = bf16[2,4,16,1536]{3,2,1,0:T(8,128)(2,1)S(1)} async-done(((bf16[2,4,16,1536]{3,2,1,0:T(8,128)(2,1)}), bf16[2,4,16,1536]{3,2,1,0:T(8,128)(2,1)S(1)}, u32[]{:S(2)}, u32[]{:S(2)}) %all-to-all-start.1) | async-done | bytes 393248 | tf_op jit(solution)/shard_map/all_to_all | solution.py:146
  (80 shorter events, 86.9 us)
Async XLA Ops:
  7.2 10.5 %copy-start = (f32[1536,8]{0,1:T(8,128)S(1)}, f32[1536,8]{0,1:T(8,128)}, u32[]{:S(2)}) copy-start(f32[1536,8]{0,1:T(8,128)} %param.23) | copy-start | bytes 147460
  7.2 9.0 %copy-start.6 = (bf16[16,2,256]{2,1,0:T(2,128)(2,1)S(1)}, bf16[16,2,256]{2,1,0:T(2,128)(2,1)}, u32[]{:S(2)}) copy-start(bf16[16,2,256]{2,1,0:T(2,128)(2,1)} %param.18) | copy-start | bytes 49156
  7.2 95.0 %all-gather.2.cloned.1.call-start = ((), (), s32[]{:S(2)}) async-start(), calls=%async_computation.3 | async-start | bytes 6684672 | tf_op jit(solution)/shard_map/all_gather | solution.py:120
  10.4 6.1 %copy-start.5 = (bf16[16,2,512,128]{3,2,1,0:T(8,128)(2,1)S(1)}, bf16[16,2,512,128]{3,2,1,0:T(8,128)(2,1)}, u32[]{:S(2)}) copy-start(bf16[16,2,512,128]{3,2,1,0:T(8,128)(2,1)} %param.20) | copy-start | bytes 12582916
  14.1 3.5 copy-start.4
  14.1 3.5 copy-start.2
  42.9 303.1 %reduce-scatter.2.cloned.1.call-start = ((), (), s32[]{:S(2)}) async-start(), calls=%async_computation.4 | async-start | bytes 6684672 | tf_op jit(solution)/shard_map/reduce_scatter | solution.py:143
  256.0 100.7 %copy-start.1 = (f32[1536,8]{0,1:T(8,128)S(1)}, f32[1536,8]{0,1:T(8,128)}, u32[]{:S(2)}) copy-start(f32[1536,8]{0,1:T(8,128)} %param.23) | copy-start | bytes 147460
  262.1 0.9 copy-start.3
  346.1 9.6 %all-to-all-start.1 = ((bf16[2,4,16,1536]{3,2,1,0:T(8,128)(2,1)}), bf16[2,4,16,1536]{3,2,1,0:T(8,128)(2,1)S(1)}, u32[]{:S(2)}, u32[]{:S(2)}) async-start(bf16[2,4,16,1536]{3,2,1,0:T(8,128)(2,1)} %bitcast.149), calls=%async_computation.2 | async-start | bytes 786432 | tf_op jit(solution)/shard_map/all_to_all | solution.py:146
Sparse Core Ops, SparseCore 0:
  43.0 59.1 all-gather.1
  262.2 83.7 reduce-scatter.1
where the time goes:
time: 366 us; the launch traced here: 364 us
  matrix products  161 us (44%)
  waiting for transfers between devices  99 us (27%)
  local copies, waits for them, and re-layouts  59.6 us (16%)
  blocking collectives  22.9 us (6%)
  between operations  14.3 us (4%)
  starting transfers between devices  3.73 us (1%)
    reduce_scatter x1, waiting for transfers between devices, per_device(): lax.psum_scatter(down_terms.astype(jnp.bfloat16), ('grp', 'tp'), scatter_...  83.1 us
    dot_general x16, matrix products, add_block(): jnp.einsum('ajcd,jdf->jacf', block, up_rows, preferred_element_type=jnp.f...  64.4 us
    dot_general x16, matrix products, add_block(): jnp.einsum('ajcd,jdf->jacf', block, gate_rows, preferred_element_type=jnp...  64.4 us
    reshape x1, local copies, waits for them, and re-layouts, per_device(): w_down.reshape(local_experts, hidden_local, tensor_count, slice_width)  49.2 us
    dot_general x1, matrix products, per_device(): jnp.einsum('jgacf,jftd->gtajcd', hidden, down_split, preferred_element_ty...  24.6 us
    psum x1, blocking collectives, per_device(): squares, logits = lax.psum((squares, partial_logits), 'tp')  13.9 us
    all_gather x1, waiting for transfers between devices, per_device(): pieces = lax.all_gather(received, ('grp', 'tp'), axis=0, tiled=True)  9.82 us
    all_to_all x1, blocking collectives, per_device(): lax.all_to_all(outgoing, 'ex', split_axis=0, concat_axis=0, tiled=True)  8.99 us
  transfers between devices with their start and end apart: 3, of which 3 were waited for; matrix products, arithmetic and copies ran while one was open for 14% of the time, Pallas kernels for 0%

commit v1 on v0

v1 whole, which is shorter than its diff:
```python
import functools

import jax
import jax.numpy as jnp
from jax import lax
from jax.experimental import pallas as pl
from jax.experimental.pallas import tpu as pltpu
from jax.sharding import PartitionSpec as P

LANES = 128


def attend(query_new, key_new, value_new, key_cache, value_cache, lengths):
    env_count, step_count, feature_count = query_new.shape
    kv_count = key_cache.shape[1]
    context = key_cache.shape[2]
    head_dim = key_cache.shape[3]
    group_size = feature_count // (kv_count * head_dim)
    queries = query_new.reshape(env_count, step_count, kv_count, group_size, head_dim)
    keys_now = key_new.reshape(env_count, step_count, kv_count, head_dim)
    values_now = value_new.reshape(env_count, step_count, kv_count, head_dim)
    score_scale = head_dim ** (-0.5)
    cached = (
        jnp.einsum("eskgd,ekcd->eskgc", queries, key_cache, preferred_element_type=jnp.float32)
        * score_scale
    )
    fresh_scores = (
        jnp.einsum("eskgd,etkd->eskgt", queries, keys_now, preferred_element_type=jnp.float32)
        * score_scale
    )
    valid_mask = (lax.broadcasted_iota(jnp.int32, (env_count, context), 1) < lengths[:, None])[
        :, None, None, None, :
    ]
    causal = (
        lax.broadcasted_iota(jnp.int32, (step_count, step_count), 1)
        <= lax.broadcasted_iota(jnp.int32, (step_count, step_count), 0)
    )[None, :, None, None, :]
    cached = jnp.where(valid_mask, cached, -1e30)
    fresh_scores = jnp.where(causal, fresh_scores, -1e30)
    row_top = jnp.maximum(jnp.max(cached, -1), jnp.max(fresh_scores, -1))[..., None]
    weight_cached = jnp.where(valid_mask, jnp.exp(cached - row_top), 0.0)
    weight_fresh = jnp.where(causal, jnp.exp(fresh_scores - row_top), 0.0)
    row_total = (jnp.sum(weight_cached, -1) + jnp.sum(weight_fresh, -1))[..., None]
    probs_cached = (weight_cached / row_total).astype(jnp.bfloat16)
    probs_fresh = (weight_fresh / row_total).astype(jnp.bfloat16)
    heads_out = jnp.einsum(
        "eskgc,ekcd->eskgd", probs_cached, value_cache, preferred_element_type=jnp.float32
    )
    heads_out = heads_out + jnp.einsum(
        "eskgt,etkd->eskgd", probs_fresh, values_now, preferred_element_type=jnp.float32
    )
    return heads_out.reshape(env_count, step_count, feature_count)


def expert_kernel(
    shards, experts_here, width, slice_width, got, gate_w, up_w, down_w, out, gate_acc, up_acc, hidden, inverse, gates
):
    step = pl.program_id(0)
    sources, _, rows, _ = got.shape
    tokens = sources * rows
    shard = lax.rem(step, shards)
    expert = lax.div(step, shards)
    first_phase = experts_here * shards

    @pl.when(step == 0)
    def _():
        info = jnp.zeros((tokens, LANES), jnp.float32)
        for k in range(shards):
            info += got[:, k, :, slice_width:].astype(jnp.float32).reshape(tokens, LANES)
        routed = got[:, 0, :, slice_width:].astype(jnp.float32).reshape(tokens, LANES)
        squares = info[:, 0:1] + info[:, 1:2] + info[:, 2:3]
        root_mean = jnp.sqrt(squares / width + 1e-05)
        difference = (info[:, 3:4] + info[:, 4:5] + info[:, 5:6]) / root_mean
        first = 1.0 / (1.0 + jnp.exp(difference))
        inverse[...] = 1.0 / root_mean
        base = lax.axis_index("ex") * experts_here
        for e in range(experts_here):
            own = (base + e).astype(jnp.float32)
            gates[e] = jnp.where(routed[:, 6:7] == own, first, 0.0) + jnp.where(
                routed[:, 7:8] == own, 1.0 - first, 0.0
            )

    @pl.when(step < first_phase)
    def _():
        block = got[:, shard, :, :slice_width].reshape(tokens, slice_width)
        gate_add = jnp.dot(block, gate_w[...], preferred_element_type=jnp.float32)
        up_add = jnp.dot(block, up_w[...], preferred_element_type=jnp.float32)

        @pl.when(shard == 0)
        def _():
            gate_acc[...] = gate_add
            up_acc[...] = up_add

        @pl.when(shard != 0)
        def _():
            gate_acc[...] += gate_add
            up_acc[...] += up_add

        @pl.when(shard == shards - 1)
        def _():
            scale = inverse[...]
            gate = gate_acc[...] * scale
            value = gate / (1.0 + jnp.exp(-gate)) * (up_acc[...] * scale) * gates[expert]
            hidden[expert] = value.astype(jnp.bfloat16)

    @pl.when(step >= first_phase)
    def _():
        total = jnp.zeros((tokens, down_w.shape[2]), jnp.float32)
        for e in range(experts_here):
            total += jnp.dot(hidden[e], down_w[e], preferred_element_type=jnp.float32)
        out[...] = total.astype(jnp.bfloat16).reshape(sources, rows, down_w.shape[2])


def run_experts(got, w_gate, w_up, w_down):
    sources, shards, rows, columns = got.shape
    experts_here, width, hidden_local = w_gate.shape
    slice_width = width // shards
    tile = 512 if slice_width % 512 == 0 else 256
    tiles = slice_width // tile
    tokens = sources * rows
    phase = experts_here * shards

    def gate_at(i):
        j = jnp.minimum(i, phase - 1)
        return (lax.div(j, shards), lax.rem(j, shards), 0)

    def down_at(i):
        return (0, 0, jnp.maximum(i - phase, 0))

    def out_at(i):
        n = jnp.maximum(i - phase, 0)
        return (0, lax.div(n, tiles), 0, lax.rem(n, tiles))

    return pl.pallas_call(
        functools.partial(expert_kernel, shards, experts_here, width, slice_width),
        out_shape=jax.ShapeDtypeStruct((sources, shards, rows, slice_width), jnp.bfloat16),
        grid=(phase + shards * tiles,),
        in_specs=[
            pl.BlockSpec((sources, shards, rows, columns), lambda i: (0, 0, 0, 0)),
            pl.BlockSpec((None, slice_width, hidden_local), gate_at),
            pl.BlockSpec((None, slice_width, hidden_local), gate_at),
            pl.BlockSpec((experts_here, hidden_local, tile), down_at),
        ],
        out_specs=pl.BlockSpec((sources, None, rows, tile), out_at),
        scratch_shapes=[
            pltpu.VMEM((tokens, hidden_local), jnp.float32),
            pltpu.VMEM((tokens, hidden_local), jnp.float32),
            pltpu.VMEM((experts_here, tokens, hidden_local), jnp.bfloat16),
            pltpu.VMEM((tokens, 1), jnp.float32),
            pltpu.VMEM((experts_here, tokens, 1), jnp.float32),
        ],
        compiler_params=pltpu.CompilerParams(vmem_limit_bytes=50 * 1024 * 1024),
        cost_estimate=pl.CostEstimate(
            flops=6 * tokens * experts_here * width * hidden_local,
            bytes_accessed=6 * experts_here * width * hidden_local + 4 * tokens * width,
            transcendentals=experts_here * tokens * hidden_local,
        ),
    )(got, w_gate, w_up, w_down)


def in_parts(value):
    high = lax.reduce_precision(value, 8, 7)
    middle = lax.reduce_precision(value - high, 8, 7)
    low = value - high - middle
    return [high, middle, low]


def per_device(
    residual,
    query_new,
    key_new,
    value_new,
    key_cache,
    value_cache,
    lengths,
    norm_gain,
    router,
    routes,
    w_gate,
    w_up,
    w_down,
):
    env_count, step_count, slice_width = residual.shape
    local_experts, width, hidden_local = w_gate.shape
    experts = router.shape[1]
    shards = lax.axis_size("tp")
    sources = lax.axis_size("grp") * lax.axis_size("ex")
    row_count = env_count * step_count
    state = residual.astype(jnp.float32) + attend(
        query_new, key_new, value_new, key_cache, value_cache, lengths
    )
    attended = state.astype(jnp.bfloat16)
    state = state.reshape(row_count, slice_width)
    squares = jnp.sum(state * state, -1)
    scaled = state * norm_gain.astype(jnp.float32)
    logits = jnp.einsum("rd,dx->rx", scaled, router, precision=lax.Precision.HIGHEST)
    pair = routes.reshape(row_count, 2)
    expert_ids = lax.broadcasted_iota(jnp.int32, (1, experts), 1)
    sign = (pair[:, 1:2] == expert_ids).astype(jnp.float32) - (
        pair[:, 0:1] == expert_ids
    ).astype(jnp.float32)
    difference = jnp.sum(sign * logits, -1)
    columns = in_parts(squares) + in_parts(difference)
    columns += [pair[:, 0].astype(jnp.float32), pair[:, 1].astype(jnp.float32)]
    info = jnp.stack(columns, axis=-1)
    info = jnp.pad(info, ((0, 0), (0, LANES - info.shape[1])))
    payload = jnp.concatenate([scaled.astype(jnp.bfloat16), info.astype(jnp.bfloat16)], axis=1)
    got = lax.all_gather(payload, ("grp", "ex", "tp"), axis=0, tiled=True)
    got = got.reshape(sources, shards, row_count, slice_width + LANES)
    terms = run_experts(got, w_gate, w_up, w_down)
    terms = terms.reshape(sources * shards * row_count, slice_width)
    mixed = lax.psum_scatter(terms, ("grp", "ex", "tp"), scatter_dimension=0, tiled=True)
    return (attended, mixed.reshape(env_count, step_count, slice_width))


def solution(mesh):
    return jax.shard_map(
        per_device,
        mesh=mesh,
        in_specs=(
            P(("grp", "ex"), None, "tp"),
            P(("grp", "ex"), None, "tp"),
            P(("grp", "ex"), None, "tp"),
            P(("grp", "ex"), None, "tp"),
            P(("grp", "ex"), "tp", None, None),
            P(("grp", "ex"), "tp", None, None),
            P(("grp", "ex")),
            P("tp"),
            P("tp", None),
            P(("grp", "ex"), None, None),
            P("ex", None, ("grp", "tp")),
            P("ex", None, ("grp", "tp")),
            P("ex", ("grp", "tp"), None),
        ),
        out_specs=(P(("grp", "ex"), None, "tp"), P(("grp", "ex"), None, "tp")),
        check_vma=False,
    )
```

time: 366 us -> 237 us (0.65)
  matrix products: 161 us -> 6.49 us
  waiting for transfers between devices: 99 us -> 162 us
  local copies, waits for them, and re-layouts: 59.6 us -> 4.83 us
  Pallas kernels: 0 us -> 45.5 us
  blocking collectives: 22.9 us -> 0 us
    dot_general x36 -> x1, matrix products: 155 us -> 0.23 us  [per_device(): jnp.einsum('rd,dx->rx', scaled, router, precision=lax.Precision.HIGHEST)]
    all_gather x1, waiting for transfers between devices: 9.82 us -> 62.6 us  [per_device(): got = lax.all_gather(payload, ('grp', 'ex', 'tp'), axis=0, tiled=True)]
    reshape x2 -> x3, local copies, waits for them, and re-layouts: 49.3 us -> 1.8 us  [the longest x1 1.57 us: per_device(): return (attended, mixed.reshape(env_count, step_count, slice_width))]
    pallas_call x0 -> x1, Pallas kernels: none -> 45.5 us  [run_experts(): pl.pallas_call(functools.partial(expert_kernel, shards, experts_here, wid...]
    reduce_scatter x1, waiting for transfers between devices: 83.1 us -> 99.7 us  [per_device(): lax.psum_scatter(terms, ('grp', 'ex', 'tp'), scatter_dimension=0, tiled=T...]
    psum x1 -> x0, blocking collectives: 13.9 us -> none  [per_device(): squares, logits = lax.psum((squares, partial_logits), 'tp')]
    all_to_all x1 -> x0, blocking collectives: 8.99 us -> none  [per_device(): lax.all_to_all(outgoing, 'ex', split_axis=0, concat_axis=0, tiled=True)]
    convert_element_type x2 -> x0, local copies, waits for them, and re-layouts: 6.2 us -> none  [the longest x1 6.1 us: per_device(): down_terms.astype(jnp.bfloat16)]
  transfers between devices with their start and end apart: 3 -> 2, of which waited for: 3 -> 2; matrix products, arithmetic and copies ran while one was open for 14% -> 0% of each run, Pallas kernels for 0% -> 0%
where the time goes in v1:
time: 237 us; the launch traced here: 236 us
  waiting for transfers between devices  162 us (68%)
  Pallas kernels  45.5 us (19%)
  between operations  14.2 us (6%)
  matrix products  6.49 us (3%)
  local copies, waits for them, and re-layouts  4.83 us (2%)
  other arithmetic  2.94 us (1%)
    reduce_scatter x1, waiting for transfers between devices, per_device(): lax.psum_scatter(terms, ('grp', 'ex', 'tp'), scatter_dimension=0, tiled=T...  99.7 us
    all_gather x1, waiting for transfers between devices, per_device(): got = lax.all_gather(payload, ('grp', 'ex', 'tp'), axis=0, tiled=True)  62.6 us
    pallas_call x1, Pallas kernels, run_experts(): pl.pallas_call(functools.partial(expert_kernel, shards, experts_here, wid...  45.5 us
  transfers between devices with their start and end apart: 2, of which 2 were waited for; matrix products, arithmetic and copies ran while one was open for 0% of the time, Pallas kernels for 0%

profile of v1, /device:TPU:0, one launch (start us, length us, event | category | flops | bytes accessed | tf_op | source)
XLA Modules:
  0.0 236.4 jit_solution(7867525767707043492)
XLA Ops:
  7.2 0.7 iota_compare_fusion.1
  8.0 0.7 convert_element_type.39
  8.7 0.8 copy.72
  9.4 0.1 reshape.133
  9.5 1.0 reshape.141
  10.5 1.6 fusion.43
  12.1 3.5 %fusion.42 = (f32[16,2,2,6]{3,1,2,0:T(2,128)S(1)}, f32[16,2,2,6,512]{4,3,1,2,0:T(8,128)S(1)}) fusion(bf16[16,2,2,6,128]{4,3,2,1,0:T(8,128)(2,1)S(1)} %reshape.141, bf16[16,2,512,128]{3,2,1,0:T(8,128)(2,1)} %param.17, pred[16,512]{1,0:T(8,128)(4,1)S(1)} %iota_compare_fusion.1), kind=kOutput, calls=%fused_computation.58 | convolution fusion | flops 50921088 | bytes 5088768 | tf_op jit(solution)/shard_map/eskgd,ekcd->eskgc/dot_general | solution.py:24
  15.6 0.2 fusion.37
  15.8 0.4 fusion.22
  16.3 0.3 fusion.33
  16.6 0.9 fusion.16
  17.6 0.1 multiply_reduce_fusion
  17.7 0.1 copy.71
  17.8 0.1 reduce_sum.43
  17.9 0.2 copy.70
  18.1 0.1 reshape.132
  18.2 0.2 fusion.21
  18.6 0.1 copy.73
  18.7 0.7 fusion.31
  19.4 62.6 %all-gather.2.cloned.1.call-done = bf16[1024,1664]{1,0:T(8,128)(2,1)} async-done(((bf16[32,1664]{1,0:T(8,128)(2,1)}), bf16[1024,1664]{1,0:T(8,128)(2,1)}) %all-gather.2.cloned.1.call-update) | async-done | bytes 3407888 | tf_op jit(solution)/shard_map/all_gather | solution.py:208
  82.0 45.5 %shard_map.140 = bf16[8,4,32,1536]{3,2,1,0:T(8,128)(2,1)} custom-call(bf16[8,4,32,1664]{3,2,1,0:T(8,128)(2,1)} %bitcast.64, bf16[4,6144,512]{2,1,0:T(8,128)(2,1)} %gate_w.1, bf16[4,6144,512]{2,1,0:T(8,128)(2,1)} %up_w.1, bf16[4,512,6144]{2,1,0:T(8,128)(2,1)} %down_w.1), custom_call_target="tpu_custom_call" | custom-call | flops 19327352832 | bytes 81788928 | tf_op jit(solution)/shard_map/pallas_call | solution.py:134
  127.6 0.7 copy.74
  128.3 99.7 %reduce-scatter.2.cloned.1.call-done = bf16[32,1536]{1,0:T(8,128)(2,1)} async-done(((bf16[1024,1536]{1,0:T(8,128)(2,1)}), bf16[32,1536]{1,0:T(8,128)(2,1)}) %reduce-scatter.2.cloned.1.call-update) | async-done | bytes 98320 | tf_op jit(solution)/shard_map/reduce_scatter | solution.py:212
  228.0 1.6 reshape.136
  (24 shorter events, 0.4 us)
Async XLA Ops:
  7.2 11.1 %copy-start = (f32[1536,8]{0,1:T(8,128)S(1)}, f32[1536,8]{0,1:T(8,128)}, u32[]{:S(2)}) copy-start(f32[1536,8]{0,1:T(8,128)} %param.21) | copy-start | bytes 147460
  7.2 9.1 %copy-start.4 = (bf16[16,2,256]{2,1,0:T(2,128)(2,1)S(1)}, bf16[16,2,256]{2,1,0:T(2,128)(2,1)}, u32[]{:S(2)}) copy-start(bf16[16,2,256]{2,1,0:T(2,128)(2,1)} %param.16) | copy-start | bytes 49156
  7.2 74.8 %all-gather.2.cloned.1.call-start = ((), (), s32[]{:S(2)}) async-start(), calls=%async_computation.1 | async-start | bytes 3514368 | tf_op jit(solution)/shard_map/all_gather | solution.py:208
  10.5 6.1 %copy-start.3 = (bf16[16,2,512,128]{3,2,1,0:T(8,128)(2,1)S(1)}, bf16[16,2,512,128]{3,2,1,0:T(8,128)(2,1)}, u32[]{:S(2)}) copy-start(bf16[16,2,512,128]{3,2,1,0:T(8,128)(2,1)} %param.18) | copy-start | bytes 12582916
  16.6 1.0 copy-start.2
  19.3 208.7 %reduce-scatter.2.cloned.1.call-start = ((), (), s32[]{:S(2)}) async-start(), calls=%async_computation.2 | async-start | bytes 3244032 | tf_op jit(solution)/shard_map/reduce_scatter | solution.py:212
  82.0 147.6 %copy-start.1 = (f32[1536,8]{0,1:T(8,128)S(1)}, f32[1536,8]{0,1:T(8,128)}, u32[]{:S(2)}) copy-start(f32[1536,8]{0,1:T(8,128)} %param.21) | copy-start | bytes 147460
Sparse Core Ops, SparseCore 0:
  19.5 62.5 all-gather.1
  127.7 100.3 reduce-scatter.1

commit v2 on v1

--- a/solution.py
+++ b/solution.py
@@ -184,7 +184,8 @@
     local_experts, width, hidden_local = w_gate.shape
     experts = router.shape[1]
     shards = lax.axis_size("tp")
-    sources = lax.axis_size("grp") * lax.axis_size("ex")
+    groups = lax.axis_size("grp")
+    owners = lax.axis_size("ex")
     row_count = env_count * step_count
     state = residual.astype(jnp.float32) + attend(
         query_new, key_new, value_new, key_cache, value_cache, lengths
@@ -205,11 +206,20 @@
     info = jnp.stack(columns, axis=-1)
     info = jnp.pad(info, ((0, 0), (0, LANES - info.shape[1])))
     payload = jnp.concatenate([scaled.astype(jnp.bfloat16), info.astype(jnp.bfloat16)], axis=1)
-    got = lax.all_gather(payload, ("grp", "ex", "tp"), axis=0, tiled=True)
-    got = got.reshape(sources, shards, row_count, slice_width + LANES)
+    blocks = [payload]
+    for r in range(1, owners):
+        blocks.append(lax.ppermute(payload, "ex", [(i, (i + r) % owners) for i in range(owners)]))
+    got = lax.all_gather(jnp.concatenate(blocks, axis=0), ("grp", "tp"), axis=0, tiled=True)
+    got = got.reshape(groups, shards, owners * row_count, slice_width + LANES)
     terms = run_experts(got, w_gate, w_up, w_down)
-    terms = terms.reshape(sources * shards * row_count, slice_width)
-    mixed = lax.psum_scatter(terms, ("grp", "ex", "tp"), scatter_dimension=0, tiled=True)
+    terms = terms.reshape(groups * shards * owners * row_count, slice_width)
+    summed = lax.psum_scatter(terms, ("grp", "tp"), scatter_dimension=0, tiled=True)
+    summed = summed.reshape(owners, row_count, slice_width)
+    mixed = summed[0].astype(jnp.float32)
+    for r in range(1, owners):
+        back = lax.ppermute(summed[r], "ex", [(i, (i - r) % owners) for i in range(owners)])
+        mixed = mixed + back.astype(jnp.float32)
+    mixed = mixed.astype(jnp.bfloat16)
     return (attended, mixed.reshape(env_count, step_count, slice_width))
 
 

time: 237 us -> 199 us (0.84)
  waiting for transfers between devices: 162 us -> 119 us
  starting transfers between devices: 0.08 us -> 4.55 us
    reduce_scatter x1, waiting for transfers between devices: 99.7 us -> 65.3 us  [per_device(): lax.psum_scatter(terms, ('grp', 'tp'), scatter_dimension=0, tiled=True)]
    all_gather x1, waiting for transfers between devices: 62.6 us -> 48.1 us  [per_device(): lax.all_gather(jnp.concatenate(blocks, axis=0), ('grp', 'tp'), axis=0, ti...]
    ppermute x0 -> x2, waiting for transfers between devices: none -> 5.36 us  [the longest x1 2.97 us: per_device(): lax.ppermute(payload, 'ex', [(i, (i + r) % owners) for i in range(owners)])]
    ppermute x0 -> x2, starting transfers between devices: none -> 4.47 us  [the longest x1 3 us: per_device(): lax.ppermute(payload, 'ex', [(i, (i + r) % owners) for i in range(owners)])]
  transfers between devices with their start and end apart: 2 -> 4, of which waited for: 2 -> 4; matrix products, arithmetic and copies ran while one was open for 0% -> 0% of each run, Pallas kernels for 0% -> 0%
where the time goes in v2:
time: 199 us; the launch traced here: 198 us
  waiting for transfers between devices  119 us (60%)
  Pallas kernels  45.5 us (23%)
  between operations  14.2 us (7%)
  matrix products  6.48 us (3%)
  local copies, waits for them, and re-layouts  4.85 us (2%)
  starting transfers between devices  4.55 us (2%)
  other arithmetic  3.92 us (2%)
    reduce_scatter x1, waiting for transfers between devices, per_device(): lax.psum_scatter(terms, ('grp', 'tp'), scatter_dimension=0, tiled=True)  65.3 us
    all_gather x1, waiting for transfers between devices, per_device(): lax.all_gather(jnp.concatenate(blocks, axis=0), ('grp', 'tp'), axis=0, ti...  48.1 us
    pallas_call x1, Pallas kernels, run_experts(): pl.pallas_call(functools.partial(expert_kernel, shards, experts_here, wid...  45.5 us
  transfers between devices with their start and end apart: 4, of which 4 were waited for; matrix products, arithmetic and copies ran while one was open for 0% of the time, Pallas kernels for 0%

profile of v2, /device:TPU:0, one launch (start us, length us, event | category | flops | bytes accessed | tf_op | source)
XLA Modules:
  0.0 198.4 jit_solution(17789624227977206204)
XLA Ops:
  7.2 0.7 iota_compare_fusion
  8.0 0.7 convert_element_type.48
  8.7 0.8 copy.72
  9.5 1.0 reshape.146
  10.5 1.6 fusion.41
  12.1 3.5 %fusion.40 = (f32[16,2,2,6]{3,1,2,0:T(2,128)S(1)}, f32[16,2,2,6,512]{4,3,1,2,0:T(8,128)S(1)}) fusion(bf16[16,2,2,6,128]{4,3,2,1,0:T(8,128)(2,1)S(1)} %reshape.146, bf16[16,2,512,128]{3,2,1,0:T(8,128)(2,1)} %param.17, pred[16,512]{1,0:T(8,128)(4,1)S(1)} %iota_compare_fusion), kind=kOutput, calls=%fused_computation.58 | convolution fusion | flops 50921088 | bytes 5088768 | tf_op jit(solution)/shard_map/eskgd,ekcd->eskgc/dot_general | solution.py:24
  15.6 0.2 fusion.35
  15.8 0.4 fusion.22
  16.3 0.3 fusion.31
  16.6 0.9 fusion.16
  17.9 0.2 copy.70
  18.2 0.2 fusion.21
  18.7 3.0 %collective-permute-start = (bf16[32,1664]{1,0:T(8,128)(2,1)S(1)}, bf16[32,1664]{1,0:T(8,128)(2,1)S(1)}, u32[]{:S(2)}, u32[]{:S(2)}) collective-permute-start(bf16[32,1664]{1,0:T(8,128)(2,1)S(1)} %pad_maximum_fusion.1), channel_id=1, source_target_pairs={{0,4},{4,0},{1,5},{5,1},{2,6},{6,2},{3,7},{7,3},{8,12},{12,8},{9,1... | collective-permute-start | bytes 319496 | tf_op jit(solution)/shard_map/ppermute | solution.py:211
  21.7 3.0 %collective-permute-done = bf16[32,1664]{1,0:T(8,128)(2,1)S(1)} collective-permute-done((bf16[32,1664]{1,0:T(8,128)(2,1)S(1)}, bf16[32,1664]{1,0:T(8,128)(2,1)S(1)}, u32[]{:S(2)}, u32[]{:S(2)}) %collective-permute-start) | collective-permute-done | bytes 106528 | tf_op jit(solution)/shard_map/ppermute | solution.py:211
  24.6 0.7 pad_maximum_fusion
  25.4 48.1 %all-gather.2.cloned.1.call-done = bf16[1024,1664]{1,0:T(8,128)(2,1)} async-done(((bf16[64,1664]{1,0:T(8,128)(2,1)}), bf16[1024,1664]{1,0:T(8,128)(2,1)}) %all-gather.2.cloned.1.call-update) | async-done | bytes 3407888 | tf_op jit(solution)/shard_map/all_gather | solution.py:212
  73.5 45.5 %shard_map.140 = bf16[4,4,64,1536]{3,2,1,0:T(8,128)(2,1)} custom-call(bf16[4,4,64,1664]{3,2,1,0:T(8,128)(2,1)} %bitcast.64, bf16[4,6144,512]{2,1,0:T(8,128)(2,1)} %gate_w.1, bf16[4,6144,512]{2,1,0:T(8,128)(2,1)} %up_w.1, bf16[4,512,6144]{2,1,0:T(8,128)(2,1)} %down_w.1), custom_call_target="tpu_custom_call" | custom-call | flops 19327352832 | bytes 81788928 | tf_op jit(solution)/shard_map/pallas_call | solution.py:134
  119.1 65.3 %reduce-scatter.2.cloned.1.call-done = bf16[64,1536]{1,0:T(8,128)(2,1)} async-done(((bf16[1024,1536]{1,0:T(8,128)(2,1)}), bf16[64,1536]{1,0:T(8,128)(2,1)}) %reduce-scatter.2.cloned.1.call-update) | async-done | bytes 196624 | tf_op jit(solution)/shard_map/reduce_scatter | solution.py:216
  184.4 0.9 slice.21
  185.3 1.5 collective-permute-start.1
  186.8 0.7 copy.74
  187.5 2.4 %collective-permute-done.1 = bf16[32,1536]{1,0:T(8,128)(2,1)S(1)} collective-permute-done((bf16[32,1536]{1,0:T(8,128)(2,1)S(1)}, bf16[32,1536]{1,0:T(8,128)(2,1)S(1)}, u32[]{:S(2)}, u32[]{:S(2)}) %collective-permute-start.1) | collective-permute-done | bytes 98336 | tf_op jit(solution)/shard_map/ppermute | solution.py:220
  189.9 0.9 add_convert_fusion
  190.8 0.7 reshape.141
  (32 shorter events, 1.0 us)
Async XLA Ops:
  7.2 11.0 %copy-start = (f32[1536,8]{0,1:T(8,128)S(1)}, f32[1536,8]{0,1:T(8,128)}, u32[]{:S(2)}) copy-start(f32[1536,8]{0,1:T(8,128)} %param.21) | copy-start | bytes 147460
  7.2 9.1 %copy-start.4 = (bf16[16,2,256]{2,1,0:T(2,128)(2,1)S(1)}, bf16[16,2,256]{2,1,0:T(2,128)(2,1)}, u32[]{:S(2)}) copy-start(bf16[16,2,256]{2,1,0:T(2,128)(2,1)} %param.16) | copy-start | bytes 49156
  7.2 66.4 %all-gather.2.cloned.1.call-start = ((), (), s32[]{:S(2)}) async-start(), calls=%async_computation.1 | async-start | bytes 3620864 | tf_op jit(solution)/shard_map/all_gather | solution.py:212
  10.5 6.1 %copy-start.3 = (bf16[16,2,512,128]{3,2,1,0:T(8,128)(2,1)S(1)}, bf16[16,2,512,128]{3,2,1,0:T(8,128)(2,1)}, u32[]{:S(2)}) copy-start(bf16[16,2,512,128]{3,2,1,0:T(8,128)(2,1)} %param.18) | copy-start | bytes 12582916
  16.6 1.0 copy-start.2
  18.7 6.0 %collective-permute-start = (bf16[32,1664]{1,0:T(8,128)(2,1)S(1)}, bf16[32,1664]{1,0:T(8,128)(2,1)S(1)}, u32[]{:S(2)}, u32[]{:S(2)}) collective-permute-start(bf16[32,1664]{1,0:T(8,128)(2,1)S(1)} %pad_maximum_fusion.1), channel_id=1, source_target_pairs={{0,4},{4,0},{1,5},{5,1},{2,6},{6,2},{3,7},{7,3},{8,12},{12,8},{9,1... | collective-permute-start | bytes 319496 | tf_op jit(solution)/shard_map/ppermute | solution.py:211
  25.4 159.0 %reduce-scatter.2.cloned.1.call-start = ((), (), s32[]{:S(2)}) async-start(), calls=%async_computation.2 | async-start | bytes 3342336 | tf_op jit(solution)/shard_map/reduce_scatter | solution.py:216
  73.5 118.0 %copy-start.1 = (f32[1536,8]{0,1:T(8,128)S(1)}, f32[1536,8]{0,1:T(8,128)}, u32[]{:S(2)}) copy-start(f32[1536,8]{0,1:T(8,128)} %param.21) | copy-start | bytes 147460
  185.3 4.6 %collective-permute-start.1 = (bf16[32,1536]{1,0:T(8,128)(2,1)S(1)}, bf16[32,1536]{1,0:T(8,128)(2,1)S(1)}, u32[]{:S(2)}, u32[]{:S(2)}) collective-permute-start(bf16[32,1536]{1,0:T(8,128)(2,1)S(1)} %slice.21), channel_id=1, source_target_pairs={{0,4},{4,0},{1,5},{5,1},{2,6},{6,2},{3,7},{7,3},{8,12},{12,8},{9,1... | collective-permute-start | bytes 294920 | tf_op jit(solution)/shard_map/ppermute | solution.py:220
Sparse Core Ops, SparseCore 0:
  25.5 47.9 all-gather.1
  119.2 65.1 reduce-scatter.1
